TPU v7x, 32 devices: a whole 2x2x4 slice. The times are simulated.
32 devices in a mesh: dp: 4 (over x, core), fsdp: 8 (over z, y).
Axes of the slice: x: 2, y: 2, z: 4, core: 2. Of those that a mesh axis runs over, the one named last changes fastest.
Arguments:
- frames: bfloat16 [51200, 640], P(('dp', 'fsdp')), may hold values from -6 to 6
- cotangent: bfloat16 [51200, 640], P(('dp', 'fsdp')), may hold values from -6 to 6
- span_starts: int32 [128, 32], P(('dp', 'fsdp')), may hold values from 0 to 390
- query_weight: bfloat16 [768, 768], P('fsdp'), may hold values from -0.25 to 0.25
- key_weight: bfloat16 [768, 768], P('fsdp'), may hold values from -0.25 to 0.25
- value_weight: bfloat16 [768, 768], P('fsdp'), may hold values from -0.25 to 0.25
- out_weight: bfloat16 [768, 768], P('fsdp'), may hold values from -3 to 3
- query_bias: bfloat16 [768], P('fsdp'), may hold values from -2.390625 to 2.390625
- value_bias: bfloat16 [768], P('fsdp'), may hold values from -2.390625 to 2.390625
- out_bias: bfloat16 [768], P('fsdp'), may hold values from -2.390625 to 2.390625
- first_gain: bfloat16 [768], P('fsdp'), may hold values from 0.3984375 to 1.59375
- first_shift: bfloat16 [768], P('fsdp'), may hold values from -2.390625 to 2.390625
- up_weight: bfloat16 [768, 3072], P('fsdp'), may hold values from -0.25 to 0.25
- up_bias: bfloat16 [3072], P('fsdp'), may hold values from -2.390625 to 2.390625
- down_weight: bfloat16 [3072, 768], P('fsdp'), may hold values from -0.15625 to 0.15625
- down_bias: bfloat16 [768], P('fsdp'), may hold values from -2.390625 to 2.390625
- second_gain: bfloat16 [768], P('fsdp'), may hold values from 0.3984375 to 1.59375
- second_shift: bfloat16 [768], P('fsdp'), may hold values from -2.390625 to 2.390625
- mask_vector: bfloat16 [768], P('fsdp'), may hold values from -5 to 5
Outputs:
- output: bfloat16 [51200, 640], P(('dp', 'fsdp'))
- frames_grad: bfloat16 [51200, 640], P(('dp', 'fsdp'))
- query_weight_grad: float32 [768, 768], P('fsdp')
- key_weight_grad: float32 [768, 768], P('fsdp')
- value_weight_grad: float32 [768, 768], P('fsdp')
- out_weight_grad: float32 [768, 768], P('fsdp')
- query_bias_grad: float32 [768], P('fsdp')
- value_bias_grad: float32 [768], P('fsdp')
- out_bias_grad: float32 [768], P('fsdp')
- first_gain_grad: float32 [768], P('fsdp')
- first_shift_grad: float32 [768], P('fsdp')
- up_weight_grad: float32 [768, 3072], P('fsdp')
- up_bias_grad: float32 [3072], P('fsdp')
- down_weight_grad: float32 [3072, 768], P('fsdp')
- down_bias_grad: float32 [768], P('fsdp')
- second_gain_grad: float32 [768], P('fsdp')
- second_shift_grad: float32 [768], P('fsdp')
- mask_vector_grad: float32 [768], P('fsdp')
Inputs may be any that keep to these rules, and one draw needn't show every extreme that they name: `span_starts`: first frame of a masked span of 10 frames within its utterance; spans may intersect.
All inputs are finite; a program needn't handle non-finite values.
Results may differ from a plain program's by a relative error of at most 0.015.
Values may be sent and summed in bfloat16 or wider, within the bound.
No kernel may reach another device: no remote copies, remote signals or barrier semaphores. Data moves between devices by JAX's collectives and lax.ppermute only.
A program may use at most 256 MiB of HBM per device.

v0:
```python
import jax
import jax.numpy as jnp
from jax import lax
from jax.sharding import PartitionSpec as P

HEADS = 10
HEAD_DIM = 64
FF = 2560
D = 640
FRAMES = 400
SPAN = 10
epsilon = 1e-05


def matmul(left, right):
    return jnp.dot(left, right, preferred_element_type=jnp.float32)


def matmul_nt(left, right):
    return lax.dot_general(
        left, right, (((1,), (1,)), ((), ())), preferred_element_type=jnp.float32
    )


def matmul_tn(left, right):
    return lax.dot_general(
        left, right, (((0,), (0,)), ((), ())), preferred_element_type=jnp.float32
    )


def layer_norm(value, gain, shift):
    center = value - jnp.mean(value, axis=-1, keepdims=True)
    spread = jnp.mean(center * center, axis=-1, keepdims=True)
    return center * lax.rsqrt(spread + epsilon) * gain + shift


def gelu_exact(value):
    return jax.nn.gelu(value, approximate=False)


def span_mask(starts):
    places = jnp.arange(FRAMES, dtype=jnp.int32)[None, :, None]
    inside = (places >= starts[:, None, :]) & (places < starts[:, None, :] + SPAN)
    return jnp.any(inside, axis=2)


def widen(grad, full_shape):
    return jnp.pad(grad, [(0, whole - part) for whole, part in zip(full_shape, grad.shape)])


def column_sum(value):
    return jnp.sum(value, axis=0, dtype=jnp.float32)


def cut_attn(gathered):
    query_w, key_w, value_w, out_w, query_b, value_b, out_b, gain_one, shift_one, mask_vec = (
        gathered
    )
    return (
        query_w[:D, :D],
        key_w[:D, :D],
        value_w[:D, :D],
        out_w[:D, :D],
        query_b[:D].astype(jnp.float32),
        value_b[:D].astype(jnp.float32),
        out_b[:D].astype(jnp.float32),
        gain_one[:D].astype(jnp.float32),
        shift_one[:D].astype(jnp.float32),
        mask_vec[:D].astype(jnp.float32),
    )


def cut_ffn(gathered):
    up_w, up_b, down_w, down_b, gain_two, shift_two = gathered
    return (
        up_w[:D, :FF],
        up_b[:FF].astype(jnp.float32),
        down_w[:FF, :D],
        down_b[:D].astype(jnp.float32),
        gain_two[:D].astype(jnp.float32),
        shift_two[:D].astype(jnp.float32),
    )


def on_device(
    frames,
    cotangent,
    span_starts,
    query_weight,
    key_weight,
    value_weight,
    out_weight,
    query_bias,
    value_bias,
    out_bias,
    first_gain,
    first_shift,
    up_weight,
    up_bias,
    down_weight,
    down_bias,
    second_gain,
    second_shift,
    mask_vector,
):
    attn_full = (
        lax.all_gather(query_weight, "fsdp", axis=0, tiled=True),
        lax.all_gather(key_weight, "fsdp", axis=0, tiled=True),
        lax.all_gather(value_weight, "fsdp", axis=0, tiled=True),
        lax.all_gather(out_weight, "fsdp", axis=0, tiled=True),
        lax.all_gather(query_bias, "fsdp", axis=0, tiled=True),
        lax.all_gather(value_bias, "fsdp", axis=0, tiled=True),
        lax.all_gather(out_bias, "fsdp", axis=0, tiled=True),
        lax.all_gather(first_gain, "fsdp", axis=0, tiled=True),
        lax.all_gather(first_shift, "fsdp", axis=0, tiled=True),
        lax.all_gather(mask_vector, "fsdp", axis=0, tiled=True),
    )
    attn_shapes = [piece.shape for piece in attn_full]
    query_w, key_w, value_w, out_w, query_b, value_b, out_b, gain_one, shift_one, mask_vec = (
        cut_attn(attn_full)
    )
    total_rows = frames.shape[0]
    utters = total_rows // FRAMES
    scale = HEAD_DIM ** (-0.5)
    masked = span_mask(span_starts).reshape(total_rows, 1)
    start_rows = jnp.where(masked, mask_vec[None, :], frames.astype(jnp.float32))
    start_low = start_rows.astype(jnp.bfloat16)
    query_rows = (matmul(start_low, query_w) + query_b).astype(jnp.bfloat16)
    key_rows = matmul(start_low, key_w).astype(jnp.bfloat16)
    value_rows = (matmul(start_low, value_w) + value_b).astype(jnp.bfloat16)
    query_heads = query_rows.reshape(utters, FRAMES, HEADS, HEAD_DIM)
    key_heads = key_rows.reshape(utters, FRAMES, HEADS, HEAD_DIM)
    value_heads = value_rows.reshape(utters, FRAMES, HEADS, HEAD_DIM)
    scores = (
        jnp.einsum("bqhd,bkhd->bhqk", query_heads, key_heads, preferred_element_type=jnp.float32)
        * scale
    )
    top = jnp.max(scores, axis=-1, keepdims=True)
    expo = jnp.exp(scores - top)
    total = jnp.sum(expo, axis=-1, keepdims=True)
    log_total = top + jnp.log(total)
    attn_prob = (expo / total).astype(jnp.bfloat16)
    mixed = jnp.einsum(
        "bhqk,bkhd->bqhd", attn_prob, value_heads, preferred_element_type=jnp.float32
    )
    mixed = mixed.reshape(total_rows, D).astype(jnp.bfloat16)
    branch_one = matmul(mixed, out_w) + out_b
    first_out, first_pull = jax.vjp(layer_norm, start_rows + branch_one, gain_one, shift_one)
    ffn_full = (
        lax.all_gather(up_weight, "fsdp", axis=0, tiled=True),
        lax.all_gather(up_bias, "fsdp", axis=0, tiled=True),
        lax.all_gather(down_weight, "fsdp", axis=0, tiled=True),
        lax.all_gather(down_bias, "fsdp", axis=0, tiled=True),
        lax.all_gather(second_gain, "fsdp", axis=0, tiled=True),
        lax.all_gather(second_shift, "fsdp", axis=0, tiled=True),
    )
    ffn_shapes = [piece.shape for piece in ffn_full]
    up_w, up_b, down_w, down_b, gain_two, shift_two = cut_ffn(ffn_full)
    first_low = first_out.astype(jnp.bfloat16)
    hidden_pre = matmul(first_low, up_w) + up_b
    hidden_act, gelu_pull = jax.vjp(gelu_exact, hidden_pre)
    hidden_low = hidden_act.astype(jnp.bfloat16)
    branch_two = matmul(hidden_low, down_w) + down_b
    result, second_pull = jax.vjp(layer_norm, first_out + branch_two, gain_two, shift_two)
    grad_two, grad_gain_two, grad_shift_two = second_pull(cotangent.astype(jnp.float32))
    grad_branch = grad_two.astype(jnp.bfloat16)
    ffn_back = cut_ffn(
        (
            lax.all_gather(up_weight, "fsdp", axis=0, tiled=True),
            lax.all_gather(up_bias, "fsdp", axis=0, tiled=True),
            lax.all_gather(down_weight, "fsdp", axis=0, tiled=True),
            lax.all_gather(down_bias, "fsdp", axis=0, tiled=True),
            lax.all_gather(second_gain, "fsdp", axis=0, tiled=True),
            lax.all_gather(second_shift, "fsdp", axis=0, tiled=True),
        )
    )
    up_w = ffn_back[0]
    down_w = ffn_back[2]
    grad_hidden = matmul_nt(grad_branch, down_w)
    (grad_pre,) = gelu_pull(grad_hidden)
    grad_pre_low = grad_pre.astype(jnp.bfloat16)
    grad_first = matmul_nt(grad_pre_low, up_w) + grad_two
    ffn_grads = (
        widen(matmul_tn(first_low, grad_pre_low), ffn_shapes[0]),
        widen(column_sum(grad_pre_low), ffn_shapes[1]),
        widen(matmul_tn(hidden_low, grad_branch), ffn_shapes[2]),
        widen(column_sum(grad_branch), ffn_shapes[3]),
        widen(grad_gain_two, ffn_shapes[4]),
        widen(grad_shift_two, ffn_shapes[5]),
    )
    grad_res, grad_gain_one, grad_shift_one = first_pull(grad_first)
    grad_attn_out = grad_res.astype(jnp.bfloat16)
    attn_back = cut_attn(
        (
            lax.all_gather(query_weight, "fsdp", axis=0, tiled=True),
            lax.all_gather(key_weight, "fsdp", axis=0, tiled=True),
            lax.all_gather(value_weight, "fsdp", axis=0, tiled=True),
            lax.all_gather(out_weight, "fsdp", axis=0, tiled=True),
            lax.all_gather(query_bias, "fsdp", axis=0, tiled=True),
            lax.all_gather(value_bias, "fsdp", axis=0, tiled=True),
            lax.all_gather(out_bias, "fsdp", axis=0, tiled=True),
            lax.all_gather(first_gain, "fsdp", axis=0, tiled=True),
            lax.all_gather(first_shift, "fsdp", axis=0, tiled=True),
            lax.all_gather(mask_vector, "fsdp", axis=0, tiled=True),
        )
    )
    query_w = attn_back[0]
    key_w = attn_back[1]
    value_w = attn_back[2]
    out_w = attn_back[3]
    grad_mixed = matmul_nt(grad_attn_out, out_w).astype(jnp.bfloat16)
    grad_mixed_heads = grad_mixed.reshape(utters, FRAMES, HEADS, HEAD_DIM)
    scores_again = (
        jnp.einsum("bqhd,bkhd->bhqk", query_heads, key_heads, preferred_element_type=jnp.float32)
        * scale
    )
    prob_again = jnp.exp(scores_again - log_total)
    grad_prob = jnp.einsum(
        "bqhd,bkhd->bhqk", grad_mixed_heads, value_heads, preferred_element_type=jnp.float32
    )
    grad_value = jnp.einsum(
        "bhqk,bqhd->bkhd",
        prob_again.astype(jnp.bfloat16),
        grad_mixed_heads,
        preferred_element_type=jnp.float32,
    )
    grad_value = grad_value.reshape(total_rows, D).astype(jnp.bfloat16)
    grad_scores = (
        prob_again * (grad_prob - jnp.sum(grad_prob * prob_again, axis=-1, keepdims=True))
    ).astype(jnp.bfloat16)
    grad_query = (
        jnp.einsum("bhqk,bkhd->bqhd", grad_scores, key_heads, preferred_element_type=jnp.float32)
        * scale
    )
    grad_query = grad_query.reshape(total_rows, D).astype(jnp.bfloat16)
    grad_key = (
        jnp.einsum("bhqk,bqhd->bkhd", grad_scores, query_heads, preferred_element_type=jnp.float32)
        * scale
    )
    grad_key = grad_key.reshape(total_rows, D).astype(jnp.bfloat16)
    grad_start = (
        matmul_nt(grad_query, query_w)
        + matmul_nt(grad_key, key_w)
        + matmul_nt(grad_value, value_w)
        + grad_res
    )
    frames_grad = jnp.where(masked, 0.0, grad_start).astype(jnp.bfloat16)
    grad_mask = jnp.sum(jnp.where(masked, grad_start, 0.0), axis=0)
    attn_grads = (
        widen(matmul_tn(start_low, grad_query), attn_shapes[0]),
        widen(matmul_tn(start_low, grad_key), attn_shapes[1]),
        widen(matmul_tn(start_low, grad_value), attn_shapes[2]),
        widen(matmul_tn(mixed, grad_attn_out), attn_shapes[3]),
        widen(column_sum(grad_query), attn_shapes[4]),
        widen(column_sum(grad_value), attn_shapes[5]),
        widen(column_sum(grad_attn_out), attn_shapes[6]),
        widen(grad_gain_one, attn_shapes[7]),
        widen(grad_shift_one, attn_shapes[8]),
        widen(grad_mask, attn_shapes[9]),
    )
    summed = lax.psum(
        (
            lax.psum_scatter(attn_grads[0], "fsdp", scatter_dimension=0, tiled=True),
            lax.psum_scatter(attn_grads[1], "fsdp", scatter_dimension=0, tiled=True),
            lax.psum_scatter(attn_grads[2], "fsdp", scatter_dimension=0, tiled=True),
            lax.psum_scatter(attn_grads[3], "fsdp", scatter_dimension=0, tiled=True),
            lax.psum_scatter(attn_grads[4], "fsdp", scatter_dimension=0, tiled=True),
            lax.psum_scatter(attn_grads[5], "fsdp", scatter_dimension=0, tiled=True),
            lax.psum_scatter(attn_grads[6], "fsdp", scatter_dimension=0, tiled=True),
            lax.psum_scatter(attn_grads[7], "fsdp", scatter_dimension=0, tiled=True),
            lax.psum_scatter(attn_grads[8], "fsdp", scatter_dimension=0, tiled=True),
            lax.psum_scatter(attn_grads[9], "fsdp", scatter_dimension=0, tiled=True),
            lax.psum_scatter(ffn_grads[0], "fsdp", scatter_dimension=0, tiled=True),
            lax.psum_scatter(ffn_grads[1], "fsdp", scatter_dimension=0, tiled=True),
            lax.psum_scatter(ffn_grads[2], "fsdp", scatter_dimension=0, tiled=True),
            lax.psum_scatter(ffn_grads[3], "fsdp", scatter_dimension=0, tiled=True),
            lax.psum_scatter(ffn_grads[4], "fsdp", scatter_dimension=0, tiled=True),
            lax.psum_scatter(ffn_grads[5], "fsdp", scatter_dimension=0, tiled=True),
        ),
        "dp",
    )
    attn_sums = summed[:10]
    ffn_sums = summed[10:]
    attn_sums = [piece for piece in attn_sums]
    ffn_sums = [piece for piece in ffn_sums]
    return (
        result.astype(jnp.bfloat16),
        frames_grad,
        attn_sums[0],
        attn_sums[1],
        attn_sums[2],
        attn_sums[3],
        attn_sums[4],
        attn_sums[5],
        attn_sums[6],
        attn_sums[7],
        attn_sums[8],
        ffn_sums[0],
        ffn_sums[1],
        ffn_sums[2],
        ffn_sums[3],
        ffn_sums[4],
        ffn_sums[5],
        attn_sums[9],
    )


def solution(mesh):
    return jax.shard_map(
        on_device,
        mesh=mesh,
        in_specs=(
            P(("dp", "fsdp"), None),
            P(("dp", "fsdp"), None),
            P(("dp", "fsdp"), None),
            P("fsdp", None),
            P("fsdp", None),
            P("fsdp", None),
            P("fsdp", None),
            P("fsdp"),
            P("fsdp"),
            P("fsdp"),
            P("fsdp"),
            P("fsdp"),
            P("fsdp", None),
            P("fsdp"),
            P("fsdp", None),
            P("fsdp"),
            P("fsdp"),
            P("fsdp"),
            P("fsdp"),
        ),
        out_specs=(
            P(("dp", "fsdp"), None),
            P(("dp", "fsdp"), None),
            P("fsdp", None),
            P("fsdp", None),
            P("fsdp", None),
            P("fsdp", None),
            P("fsdp"),
            P("fsdp"),
            P("fsdp"),
            P("fsdp"),
            P("fsdp"),
            P("fsdp", None),
            P("fsdp"),
            P("fsdp", None),
            P("fsdp"),
            P("fsdp"),
            P("fsdp"),
            P("fsdp"),
        ),
        check_vma=False,
    )
```

profile of v0, /device:TPU:0, one launch (start us, length us, event | category | flops | bytes accessed | tf_op | source)
XLA Modules:
  0.0 1117.5 jit_solution(11925511347061986627)
XLA Ops:
  23.0 39.2 %all-reduce.38 = (bf16[768]{0:T(1024)(128)(2,1)S(1)}, bf16[768]{0:T(1024)(128)(2,1)S(1)}, bf16[768]{0:T(1024)(128)(2,1)S(1)}, bf16[768]{0:T(1024)(128)(2,1)S(1)}...) all-reduce(bf16[768]{0:T(1024)(128)(2,1)S(1)} %dynamic-update-slice, ...), channel_id=1, replica_groups=mesh['dp'=4,'fsdp'=8] {'fsdp'}, use_global_device_ids=true, to_apply=%add.16 | all-reduce | flops 6912 | bytes 27648
  62.2 25.9 %all-gather = bf16[8,1,384]{2,1,0:T(2,128)(2,1)S(1)} all-gather(bf16[1,1,384]{2,1,0:T(2,128)(2,1)S(1)} %reshape.175), channel_id=1, replica_groups=mesh['dp'=4,'fsdp'=8] {'fsdp'}, dimensions={0}, use_global_device_ids=true | all-gather | bytes 6912 | tf_op jit(solution)/shard_map/all_gather | solution.py:151
  116.0 22.1 %all-gather.12.cloned.1.call-done = bf16[768,768]{1,0:T(8,128)(2,1)} async-done(((bf16[96,768]{1,0:T(8,128)(2,1)}), bf16[768,768]{1,0:T(8,128)(2,1)}) %all-gather.12.cloned.1.call-update) | async-done | bytes 1179664 | tf_op jit(solution)/shard_map/all_gather | solution.py:108
  144.5 7.9 reshape.146
  152.4 15.5 %multiply_reduce_fusion.1 = (f32[4,10,400]{2,1,0:T(8,128)S(1)}, f32[4,10,400,400]{2,3,1,0:T(8,128)}) fusion(bf16[4,400,10,64]{1,0,3,2:T(4,128)(2,1)S(1)} %reshape.146, bf16[4,400,10,64]{1,0,3,2:T(4,128)(2,1)} %reshape.145), kind=kOutput, calls=%fused_computation.6 | convolution fusion | flops 831984000 | bytes 29760000 | tf_op jit(solution)/shard_map/bqhd,bkhd->bhqk/dot_general | solution.py:135
  167.9 14.0 %fusion = f32[4,10,400]{2,1,0:T(8,128)S(1)} fusion(f32[4,10,400,400]{2,3,1,0:T(8,128)} %get-tuple-element.73, f32[4,10,400]{2,1,0:T(8,128)S(1)} %get-tuple-element.72), kind=kLoop, calls=%fused_computation.5 | loop fusion | flops 19184000 | bytes 25728000 | tf_op jit(solution)/shard_map/reduce_sum | solution.py:140
  182.0 16.0 %convert_bitcast_fusion = bf16[4,400,10,64]{1,3,2,0:T(8,128)(2,1)} fusion(f32[4,10,400,400]{2,3,1,0:T(8,128)} %get-tuple-element.73, f32[4,10,400]{2,1,0:T(8,128)S(1)} %fusion, f32[4,10,400]{2,1,0:T(8,128)S(1)} %get-tuple-element.72, bf16[4,400,10,64]{1,0,3,2:T(4,128)(2,1)S(1)} %copy-done.8), kind=kOutput, calls=%fused_computation.72 | convolution fusion | flops 845824000 | bytes 29824000 | tf_op jit(solution)/shard_map/bhqk,bkhd->bqhd/dot_general | solution.py:143
  213.5 47.2 %all-gather.16.cloned.1.call-done = bf16[768,3072]{1,0:T(8,128)(2,1)} async-done(((bf16[96,3072]{1,0:T(8,128)(2,1)}), bf16[768,3072]{1,0:T(8,128)(2,1)}) %all-gather.16.cloned.1.call-update) | async-done | bytes 4718608 | tf_op jit(solution)/shard_map/all_gather | solution.py:150
  260.8 46.6 %multiply_convert_fusion.1 = (bf16[1600,2560]{1,0:T(8,128)(2,1)}, f32[1600,2560]{1,0:T(8,128)}, f32[1600,2560]{1,0:T(8,128)}) fusion(f32[2560]{0:T(1024)S(1)} %slice_convert_fusion, bf16[768,3072]{1,0:T(8,128)(2,1)} %all-gather.16.cloned.1.call-done, f32[1600,640]{1,0:T(8,128)} %copy-done.5, f32[640]{0:T(1024)S(1)} %get-tuple-element.93, ...), kind=kOutput, calls=%fused_computation.14 | convolution fusion | flops 5518336000 | bytes 48360960 | tf_op jit(solution)/shard_map/dot_general | solution.py:16
  307.4 33.5 %all-gather.18.cloned.1.call-done = bf16[3072,768]{1,0:T(8,128)(2,1)} async-done(((bf16[384,768]{1,0:T(8,128)(2,1)}), bf16[3072,768]{1,0:T(8,128)(2,1)}) %all-gather.18.cloned.1.call-update) | async-done | bytes 4718608 | tf_op jit(solution)/shard_map/all_gather | solution.py:152
  340.9 12.8 %fusion.81 = (f32[1600]{0:T(1024)S(1)}, f32[1600,640]{1,0:T(8,128)S(1)}) fusion(f32[640]{0:T(1024)S(1)} %copy-done.34, bf16[1600,2560]{1,0:T(8,128)(2,1)} %get-tuple-element.67, bf16[3072,768]{1,0:T(8,128)(2,1)} %all-gather.18.cloned.1.call-done, f32[640]{0:T(1024)S(1)} %get-tuple-element.93, f32[640]{0:T(1024)S(1)} %slice_convert_fusion.5, ...), kind=kOutput, calls=%fused_computation.132 | convolution fusion | flops 5250046464 | bytes 19687680 | tf_op jit(solution)/shard_map/dot_general | solution.py:16
  363.5 21.7 %convert_reduce_fusion = (f32[2560]{0:T(1024)}, bf16[1600,2560]{1,0:T(8,128)(2,1)}) fusion(f32[1600,2560]{1,0:T(8,128)} %get-tuple-element.68, bf16[1600,640]{1,0:T(8,128)(2,1)S(1)} %get-tuple-element.60, bf16[3072,768]{1,0:T(8,128)(2,1)} %all-gather.18.cloned.1.call-done, f32[1600,2560]{1,0:T(8,128)} %get-tuple-element.76, f32[2560]{0:T(1024)S(1)} %slice_convert_fusion), kind=kOutput, calls=%fused_computation.11 | convolution fusion | flops 5312509440 | bytes 46305280 | tf_op jit(solution)/shard_map/dot_general | solution.py:20
  385.2 14.5 %multiply_reduce_fusion.2 = (f32[640]{0:T(1024)S(1)}, f32[1600]{0:T(1024)S(1)}, f32[640]{0:T(1024)S(1)}, f32[1600,640]{1,0:T(8,128)S(1)}) fusion(f32[1600,640]{1,0:T(8,128)} %copy-done.5, f32[1600]{0:T(1024)S(1)} %fusion.60, f32[1600]{0:T(1024)S(1)} %broadcast_multiply_fusion.1, f32[640]{0:T(1024)S(1)} %slice_convert_fusion.5, f32[1600,640]{1,0:T(8,128)} %copy-done.7, ...), kind=kOutput, calls=%fused_computation.45 | convolution fusion | flops 5253117440 | bytes 23790080 | tf_op jit(solution)/shard_map/dot_general | solution.py:20
  414.8 7.9 reshape.147
  422.8 15.7 %convert_reduce_fusion.2 = (f32[10,64]{1,0:T(8,128)S(1)}, bf16[4,10,64,400]{3,2,1,0:T(8,128)(2,1)}) fusion(f32[4,10,400,400]{2,3,1,0:T(8,128)} %get-tuple-element.73, f32[4,10,400]{2,1,0:T(8,128)S(1)} %log_add_fusion, bf16[4,400,10,64]{1,0,3,2:T(4,128)(2,1)S(1)} %reshape.147), kind=kOutput, calls=%fused_computation.35 | convolution fusion | flops 841471360 | bytes 29762560 | tf_op jit(solution)/shard_map/bhqk,bqhd->bkhd/dot_general | solution.py:221
  438.4 5.4 copy.108
  443.8 6.0 convert_element_type.198
  456.0 25.6 %multiply_reduce_fusion = (f32[4,10,400]{2,1,0:T(8,128)S(1)}, f32[4,10,400,400]{2,3,1,0:T(8,128)}) fusion(f32[4,10,400,400]{2,3,1,0:T(8,128)} %get-tuple-element.73, f32[4,10,400]{2,1,0:T(8,128)S(1)} %log_add_fusion, bf16[4,400,10,64]{1,0,3,2:T(4,128)(2,1)} %reshape.144, bf16[4,400,10,64]{1,0,3,2:T(4,128)(2,1)S(1)} %reshape.147), kind=kOutput, calls=%fused_computation.1 | convolution fusion | flops 844784000 | bytes 55424000 | tf_op jit(solution)/shard_map/bqhd,bkhd->bhqk/dot_general | solution.py:218
  481.6 28.0 %multiply_convert_fusion = bf16[4,10,400,400]{2,3,1,0:T(8,128)(2,1)} fusion(f32[4,10,400,400]{2,3,1,0:T(8,128)} %get-tuple-element.81, f32[4,10,400,400]{2,3,1,0:T(8,128)} %get-tuple-element.73, f32[4,10,400]{2,1,0:T(8,128)S(1)} %get-tuple-element.80, f32[4,10,400]{2,1,0:T(8,128)S(1)} %log_add_fusion), kind=kLoop, calls=%fused_computation | loop fusion | flops 32000000 | bytes 64128000 | tf_op jit(solution)/shard_map/convert_element_type | solution.py:230
  509.7 8.7 fusion.24
  531.1 9.0 convert_reduce_fusion.3
  551.9 10.6 fusion.64
  568.9 9.9 fusion.83
  584.6 34.2 %reduce-scatter.9.cloned.1.call-done = f32[96,768]{1,0:T(8,128)} async-done(((f32[768,768]{1,0:T(8,128)}), f32[96,768]{1,0:T(8,128)}) %reduce-scatter.9.cloned.1.call-update) | async-done | bytes 294928 | tf_op jit(solution)/shard_map/reduce_scatter | solution.py:264
  618.9 71.5 %reduce-scatter.7.cloned.1.call-done = f32[96,768]{1,0:T(8,128)} async-done(((f32[768,768]{1,0:T(8,128)}), f32[96,768]{1,0:T(8,128)}) %reduce-scatter.7.cloned.1.call-update) | async-done | bytes 294928 | tf_op jit(solution)/shard_map/reduce_scatter | solution.py:263
  690.3 166.1 %reduce-scatter.15.cloned.1.call-done = f32[96,3072]{1,0:T(8,128)} async-done(((f32[768,3072]{1,0:T(8,128)}), f32[96,3072]{1,0:T(8,128)}) %reduce-scatter.15.cloned.1.call-update) | async-done | bytes 1179664 | tf_op jit(solution)/shard_map/reduce_scatter | solution.py:273
  856.4 166.1 %reduce-scatter.17.cloned.1.call-done = f32[384,768]{1,0:T(8,128)} async-done(((f32[3072,768]{1,0:T(8,128)}), f32[384,768]{1,0:T(8,128)}) %reduce-scatter.17.cloned.1.call-update) | async-done | bytes 1179664 | tf_op jit(solution)/shard_map/reduce_scatter | solution.py:275
  1022.6 5.9 fusion.50
  1032.8 6.7 select_convert_fusion
  1039.9 35.3 %all-reduce.35 = (f32[768]{0:T(1024)S(1)}, f32[768]{0:T(1024)S(1)}, f32[768]{0:T(1024)S(1)}, f32[768]{0:T(1024)S(1)}, f32[768]{0:T(1024)S(1)}, /*index=5*/f32[30...) all-reduce(f32[768]{0:T(1024)S(1)} %pad.57, ...), channel_id=6, replica_groups=mesh['dp'=4,'fsdp'=8] {'fsdp'}, use_global_device_ids=true, to_apply=%region_21.22.clone | all-reduce | flops 9984 | bytes 79872
  1075.9 7.0 all-reduce.36
  1082.9 17.5 %all-reduce.41.cloned.1.call-done = (f32[96,768]{1,0:T(8,128)}, f32[96,768]{1,0:T(8,128)}, f32[96,768]{1,0:T(8,128)}, f32[96,768]{1,0:T(8,128)}, f32[96,3072]{1,0:T(8,128)}, /*index=5*/f32[384,768]{1,0:T(8,128)}) async-done(((f32[96,768]{1,0:T(8,128)}, f32[96,768]{1,0:T(8,128)}, f32[96,768]{1,0:T(8,128)}, f32[96,768]{1,0:T(8,128)}, f32[96,3072]{1,0:T(8,128)}, /*index=5*/f32[384,768]{1,0:T(8,128)}), ...) | async-done | bytes 3538960 | tf_op jit(solution)/shard_map/psum | solution.py:261
  (211 shorter events, 146.6 us)
Async XLA Ops:
  7.2 82.3 %all-gather.8.cloned.1.call-start = ((), (), s32[]{:S(2)}) async-start(), calls=%async_computation.6 | async-start | bytes 1327104 | tf_op jit(solution)/shard_map/all_gather | solution.py:109
  7.9 95.0 %all-gather.10.cloned.1.call-start = ((), (), s32[]{:S(2)}) async-start(), calls=%async_computation.7 | async-start | bytes 1327104 | tf_op jit(solution)/shard_map/all_gather | solution.py:107
  8.7 129.4 %all-gather.12.cloned.1.call-start = ((), (), s32[]{:S(2)}) async-start(), calls=%async_computation.8 | async-start | bytes 1327104 | tf_op jit(solution)/shard_map/all_gather | solution.py:108
  9.4 195.8 %all-gather.14.cloned.1.call-start = ((), (), s32[]{:S(2)}) async-start(), calls=%async_computation.9 | async-start | bytes 1327104 | tf_op jit(solution)/shard_map/all_gather | solution.py:110
  10.0 250.8 %all-gather.16.cloned.1.call-start = ((), (), s32[]{:S(2)}) async-start(), calls=%async_computation.10 | async-start | bytes 5308416 | tf_op jit(solution)/shard_map/all_gather | solution.py:150
  10.6 330.3 %all-gather.18.cloned.1.call-start = ((), (), s32[]{:S(2)}) async-start(), calls=%async_computation.11 | async-start | bytes 5308416 | tf_op jit(solution)/shard_map/all_gather | solution.py:152
  11.1 573.4 %reduce-scatter.13.cloned.1.call-start = ((), (), s32[]{:S(2)}) async-start(), calls=%async_computation.15 | async-start | bytes 2654208 | tf_op jit(solution)/shard_map/reduce_scatter | solution.py:266
  13.5 191.7 %copy-start.25 = (pred[1600]{0:T(1024)(128)(4,1)}, pred[1600]{0:T(1024)(128)(4,1)S(1)}, u32[]{:S(2)}) copy-start(pred[1600]{0:T(1024)(128)(4,1)S(1)} %broadcast_in_dim.36) | copy-start | bytes 4804
  62.2 143.0 %copy-start.35 = (f32[640]{0:T(1024)}, f32[640]{0:T(1024)S(1)}, u32[]{:S(2)}) copy-start(f32[640]{0:T(1024)S(1)} %slice_convert_fusion.9) | copy-start | bytes 7684
  88.9 252.0 %copy-start.32 = (f32[640]{0:T(1024)}, f32[640]{0:T(1024)S(1)}, u32[]{:S(2)}) copy-start(f32[640]{0:T(1024)S(1)} %get-tuple-element.93) | copy-start | bytes 7684
  152.4 15.5 %copy-start.2 = (bf16[4,400,10,64]{1,0,3,2:T(4,128)(2,1)}, bf16[4,400,10,64]{1,0,3,2:T(4,128)(2,1)S(1)}, u32[]{:S(2)}) copy-start(bf16[4,400,10,64]{1,0,3,2:T(4,128)(2,1)S(1)} %reshape.146) | copy-start | bytes 6144004
  167.9 14.0 %copy-start.16 = (f32[4,10,400]{2,1,0:T(8,128)}, f32[4,10,400]{2,1,0:T(8,128)S(1)}, u32[]{:S(2)}) copy-start(f32[4,10,400]{2,1,0:T(8,128)S(1)} %get-tuple-element.72) | copy-start | bytes 192004
  167.9 14.1 %copy-start.8 = (bf16[4,400,10,64]{1,0,3,2:T(4,128)(2,1)S(1)}, bf16[4,400,10,64]{1,0,3,2:T(4,128)(2,1)}, u32[]{:S(2)}) copy-start(bf16[4,400,10,64]{1,0,3,2:T(4,128)(2,1)} %reshape.144) | copy-start | bytes 6144004
  181.9 16.0 %copy-start.20 = (f32[4,10,400]{2,1,0:T(8,128)}, f32[4,10,400]{2,1,0:T(8,128)S(1)}, u32[]{:S(2)}) copy-start(f32[4,10,400]{2,1,0:T(8,128)S(1)} %fusion) | copy-start | bytes 192004
  260.8 80.1 %copy-start.34 = (f32[640]{0:T(1024)S(1)}, f32[640]{0:T(1024)}, u32[]{:S(2)}) copy-start(f32[640]{0:T(1024)} %get-tuple-element.92) | copy-start | bytes 7684
  363.5 21.7 %copy-start.13 = (bf16[1600,640]{1,0:T(8,128)(2,1)}, bf16[1600,640]{1,0:T(8,128)(2,1)S(1)}, u32[]{:S(2)}) copy-start(bf16[1600,640]{1,0:T(8,128)(2,1)S(1)} %get-tuple-element.60) | copy-start | bytes 6144004
  385.2 14.5 %copy-start.23 = (f32[1600]{0:T(1024)S(1)}, f32[1600]{0:T(1024)}, u32[]{:S(2)}) copy-start(f32[1600]{0:T(1024)} %copy-done.22) | copy-start | bytes 19204
  385.2 14.6 %copy-start.6 = (f32[1600,640]{1,0:T(8,128)S(1)}, f32[1600,640]{1,0:T(8,128)}, u32[]{:S(2)}) copy-start(f32[1600,640]{1,0:T(8,128)} %copy-done.5) | copy-start | bytes 12288004
  408.2 176.4 %reduce-scatter.11.cloned.1.call-start = ((), (), s32[]{:S(2)}) async-start(), calls=%async_computation.14 | async-start | bytes 2654208 | tf_op jit(solution)/shard_map/reduce_scatter | solution.py:265
  438.4 11.3 %copy-start.26 = (pred[1600]{0:T(1024)(128)(4,1)S(1)}, pred[1600]{0:T(1024)(128)(4,1)}, u32[]{:S(2)}) copy-start(pred[1600]{0:T(1024)(128)(4,1)} %copy-done.25) | copy-start | bytes 4804
  438.4 11.3 %copy-start.36 = (f32[640]{0:T(1024)S(1)}, f32[640]{0:T(1024)}, u32[]{:S(2)}) copy-start(f32[640]{0:T(1024)} %copy-done.35) | copy-start | bytes 7684
  456.0 162.9 %reduce-scatter.9.cloned.1.call-start = ((), (), s32[]{:S(2)}) async-start(), calls=%async_computation.13 | async-start | bytes 2654208 | tf_op jit(solution)/shard_map/reduce_scatter | solution.py:264
  481.6 28.0 %copy-start.4 = (bf16[4,400,10,64]{1,0,3,2:T(4,128)(2,1)S(1)}, bf16[4,400,10,64]{1,0,3,2:T(4,128)(2,1)}, u32[]{:S(2)}) copy-start(bf16[4,400,10,64]{1,0,3,2:T(4,128)(2,1)} %reshape.145) | copy-start | bytes 6144004
  530.2 160.2 %reduce-scatter.7.cloned.1.call-start = ((), (), s32[]{:S(2)}) async-start(), calls=%async_computation.12 | async-start | bytes 2654208 | tf_op jit(solution)/shard_map/reduce_scatter | solution.py:263
  551.9 304.5 %reduce-scatter.15.cloned.1.call-start = ((), (), s32[]{:S(2)}) async-start(), calls=%async_computation.16 | async-start | bytes 10616832 | tf_op jit(solution)/shard_map/reduce_scatter | solution.py:273
  567.4 455.1 %reduce-scatter.17.cloned.1.call-start = ((), (), s32[]{:S(2)}) async-start(), calls=%async_computation.17 | async-start | bytes 10616832 | tf_op jit(solution)/shard_map/reduce_scatter | solution.py:275
  583.2 517.3 %all-reduce.41.cloned.1.call-start = ((), (), s32[]{:S(2)}) async-start(), calls=%async_computation.18 | async-start | bytes 7077888 | tf_op jit(solution)/shard_map/psum | solution.py:261
  1022.5 6.0 copy-start.29
  1022.5 6.0 copy-start.31
  1022.5 6.0 copy-start.30
  1022.6 6.2 copy-start.11
  1100.5 9.2 copy-start.18
  (18 other events, 50.0 us)
Sparse Core Ops, SparseCore 0:
  10.2 43.8 all-gather.7
  56.3 39.6 all-gather.9
  98.2 39.8 all-gather.11
  140.1 39.8 all-gather.13
  182.0 78.6 all-gather.15
  262.8 78.0 all-gather.17
  408.3 67.1 reduce-scatter.12
  479.0 68.0 reduce-scatter.10
  550.6 68.2 reduce-scatter.8
  622.2 68.0 reduce-scatter.6
  693.9 162.4 reduce-scatter.14
  859.9 162.5 reduce-scatter.16
  1025.3 75.1 all-reduce.40
where the time goes:
time: 1120 us
  waiting for transfers between devices  562 us (50%)
  matrix products  261 us (23%)
  local copies, waits for them, and re-layouts  114 us (10%)
  blocking collectives  107 us (10%)
  other arithmetic  55 us (5%)
  between operations  16.8 us (2%)
    reduce_scatter x1, waiting for transfers between devices, on_device(): lax.psum_scatter(ffn_grads[0], 'fsdp', scatter_dimension=0, tiled=True)  166 us
    reduce_scatter x1, waiting for transfers between devices, on_device(): lax.psum_scatter(ffn_grads[2], 'fsdp', scatter_dimension=0, tiled=True)  166 us
    dot_general x6, matrix products, matmul(): return jnp.dot(left, right, preferred_element_type=jnp.float32)  78.6 us
    unnamed x2, blocking collectives  74.5 us
    reduce_scatter x1, waiting for transfers between devices, on_device(): lax.psum_scatter(attn_grads[0], 'fsdp', scatter_dimension=0, tiled=True)  71.5 us
    dot_general x6, matrix products, matmul_nt(): lax.dot_general(left, right, (((1,), (1,)), ((), ())), preferred_element_...  56.2 us
    all_gather x1, waiting for transfers between devices, on_device(): lax.all_gather(up_weight, 'fsdp', axis=0, tiled=True)  47.2 us
    dot_general x6, matrix products, matmul_tn(): lax.dot_general(left, right, (((0,), (0,)), ((), ())), preferred_element_...  36.2 us
  transfers between devices with their start and end apart: 13, of which 8 were waited for; matrix products, arithmetic and copies ran while one was open for 31% of the time, Pallas kernels for 0%

commit v1 on v0

--- a/solution.py
+++ b/solution.py
@@ -10,6 +10,18 @@
 FRAMES = 400
 SPAN = 10
 epsilon = 1e-05
+
+
+def collect(x, axis, dim):
+    ways, here, step = (lax.axis_size(axis), lax.axis_index(axis), x.shape[dim])
+    line, have = (x, 1)
+    while have < ways:
+        line = jnp.concatenate(
+            [line, lax.ppermute(line, axis, [(d, (d - have) % ways) for d in range(ways)])],
+            axis=dim,
+        )
+        have = 2 * have
+    return jnp.roll(line, here * step, axis=dim)
 
 
 def matmul(left, right):
@@ -148,7 +160,7 @@
     first_out, first_pull = jax.vjp(layer_norm, start_rows + branch_one, gain_one, shift_one)
     ffn_full = (
         lax.all_gather(up_weight, "fsdp", axis=0, tiled=True),
-        lax.all_gather(up_bias, "fsdp", axis=0, tiled=True),
+        collect(up_bias, "fsdp", 0),
         lax.all_gather(down_weight, "fsdp", axis=0, tiled=True),
         lax.all_gather(down_bias, "fsdp", axis=0, tiled=True),
         lax.all_gather(second_gain, "fsdp", axis=0, tiled=True),

time: 1120 us -> 1120 us (level)
  blocking collectives: 107 us -> 75.8 us
  waiting for transfers between devices: 562 us -> 584 us
    all_gather x1 -> x0, blocking collectives: 25.9 us -> none  [on_device(): lax.all_gather(up_bias, 'fsdp', axis=0, tiled=True)]
    unnamed x111 -> x116, local copies, waits for them, and re-layouts: 31.1 us -> 33 us
  transfers between devices with their start and end apart: 13 -> 16, of which waited for: 8 -> 11; matrix products, arithmetic and copies ran while one was open for 31% -> 31% of each run, Pallas kernels for 0% -> 0%
where the time goes in v1:
time: 1120 us
  waiting for transfers between devices  584 us (52%)
  matrix products  261 us (23%)
  local copies, waits for them, and re-layouts  116 us (10%)
  blocking collectives  75.8 us (7%)
  other arithmetic  56.3 us (5%)
  between operations  16.8 us (2%)
    reduce_scatter x1, waiting for transfers between devices, on_device(): lax.psum_scatter(ffn_grads[0], 'fsdp', scatter_dimension=0, tiled=True)  166 us
    reduce_scatter x1, waiting for transfers between devices, on_device(): lax.psum_scatter(ffn_grads[2], 'fsdp', scatter_dimension=0, tiled=True)  166 us
    dot_general x6, matrix products, matmul(): return jnp.dot(left, right, preferred_element_type=jnp.float32)  78.1 us
    reduce_scatter x1, waiting for transfers between devices, on_device(): lax.psum_scatter(attn_grads[0], 'fsdp', scatter_dimension=0, tiled=True)  71.4 us
    unnamed x2, blocking collectives  68.8 us
    dot_general x6, matrix products, matmul_nt(): lax.dot_general(left, right, (((1,), (1,)), ((), ())), preferred_element_...  56.3 us
    all_gather x1, waiting for transfers between devices, on_device(): lax.all_gather(up_weight, 'fsdp', axis=0, tiled=True)  46.6 us
    dot_general x6, matrix products, matmul_tn(): lax.dot_general(left, right, (((0,), (0,)), ((), ())), preferred_element_...  36.2 us
  transfers between devices with their start and end apart: 16, of which 11 were waited for; matrix products, arithmetic and copies ran while one was open for 31% of the time, Pallas kernels for 0%

profile of v1, /device:TPU:0, one launch (start us, length us, event | category | flops | bytes accessed | tf_op | source)
XLA Modules:
  0.0 1117.4 jit_solution(13873584803537019782)
XLA Ops:
  10.6 6.1 collective-permute-start
  26.3 33.5 %all-reduce.38 = (bf16[768]{0:T(1024)(128)(2,1)S(1)}, bf16[768]{0:T(1024)(128)(2,1)S(1)}, bf16[768]{0:T(1024)(128)(2,1)S(1)}, bf16[768]{0:T(1024)(128)(2,1)S(1)}...) all-reduce(bf16[768]{0:T(1024)(128)(2,1)S(1)} %dynamic-update-slice, ...), channel_id=1, replica_groups=mesh['dp'=4,'fsdp'=8] {'fsdp'}, use_global_device_ids=true, to_apply=%add.16 | all-reduce | flops 6912 | bytes 27648
  85.5 10.8 all-gather.9.cloned.1.call-done
  109.4 29.0 %all-gather.11.cloned.1.call-done = bf16[768,768]{1,0:T(8,128)(2,1)} async-done(((bf16[96,768]{1,0:T(8,128)(2,1)}), bf16[768,768]{1,0:T(8,128)(2,1)}) %all-gather.11.cloned.1.call-update) | async-done | bytes 1179664 | tf_op jit(solution)/shard_map/all_gather | solution.py:120
  144.8 8.1 reshape.146
  152.9 15.4 %multiply_reduce_fusion.1 = (f32[4,10,400]{2,1,0:T(8,128)S(1)}, f32[4,10,400,400]{2,3,1,0:T(8,128)}) fusion(bf16[4,400,10,64]{1,0,3,2:T(4,128)(2,1)S(1)} %reshape.146, bf16[4,400,10,64]{1,0,3,2:T(4,128)(2,1)} %reshape.145), kind=kOutput, calls=%fused_computation.6 | convolution fusion | flops 831984000 | bytes 29760000 | tf_op jit(solution)/shard_map/bqhd,bkhd->bhqk/dot_general | solution.py:147
  168.3 14.0 %fusion = f32[4,10,400]{2,1,0:T(8,128)S(1)} fusion(f32[4,10,400,400]{2,3,1,0:T(8,128)} %get-tuple-element.73, f32[4,10,400]{2,1,0:T(8,128)S(1)} %get-tuple-element.72), kind=kLoop, calls=%fused_computation.5 | loop fusion | flops 19184000 | bytes 25728000 | tf_op jit(solution)/shard_map/reduce_sum | solution.py:152
  182.3 16.0 %convert_bitcast_fusion = bf16[4,400,10,64]{1,3,2,0:T(8,128)(2,1)} fusion(f32[4,10,400,400]{2,3,1,0:T(8,128)} %get-tuple-element.73, f32[4,10,400]{2,1,0:T(8,128)S(1)} %fusion, f32[4,10,400]{2,1,0:T(8,128)S(1)} %get-tuple-element.72, bf16[4,400,10,64]{1,0,3,2:T(4,128)(2,1)S(1)} %copy-done.8), kind=kOutput, calls=%fused_computation.72 | convolution fusion | flops 845824000 | bytes 29824000 | tf_op jit(solution)/shard_map/bhqk,bkhd->bqhd/dot_general | solution.py:155
  214.4 46.6 %all-gather.15.cloned.1.call-done = bf16[768,3072]{1,0:T(8,128)(2,1)} async-done(((bf16[96,3072]{1,0:T(8,128)(2,1)}), bf16[768,3072]{1,0:T(8,128)(2,1)}) %all-gather.15.cloned.1.call-update) | async-done | bytes 4718608 | tf_op jit(solution)/shard_map/all_gather | solution.py:162
  261.0 46.2 %multiply_convert_fusion.1 = (bf16[1600,2560]{1,0:T(8,128)(2,1)}, f32[1600,2560]{1,0:T(8,128)}, f32[1600,2560]{1,0:T(8,128)}) fusion(f32[2560]{0:T(1024)S(1)} %dynamic-slice_convert_fusion, bf16[768,3072]{1,0:T(8,128)(2,1)} %all-gather.15.cloned.1.call-done, f32[1600,640]{1,0:T(8,128)} %copy-done.5, f32[640]{0:T(1024)S(1)} %get-tuple-element.92, ...), kind=kOutput, calls=%fused_computation.14 | convolution fusion | flops 5518336000 | bytes 48360960 | tf_op jit(solution)/shard_map/dot_general | solution.py:28
  307.2 33.9 %all-gather.17.cloned.1.call-done = bf16[3072,768]{1,0:T(8,128)(2,1)} async-done(((bf16[384,768]{1,0:T(8,128)(2,1)}), bf16[3072,768]{1,0:T(8,128)(2,1)}) %all-gather.17.cloned.1.call-update) | async-done | bytes 4718608 | tf_op jit(solution)/shard_map/all_gather | solution.py:164
  341.1 12.8 %fusion.81 = (f32[1600]{0:T(1024)S(1)}, f32[1600,640]{1,0:T(8,128)S(1)}) fusion(f32[640]{0:T(1024)S(1)} %copy-done.36, bf16[1600,2560]{1,0:T(8,128)(2,1)} %get-tuple-element.67, bf16[3072,768]{1,0:T(8,128)(2,1)} %all-gather.17.cloned.1.call-done, f32[640]{0:T(1024)S(1)} %get-tuple-element.92, f32[640]{0:T(1024)S(1)} %get-tuple-element.93, ...), kind=kOutput, calls=%fused_computation.134 | convolution fusion | flops 5250046464 | bytes 19687680 | tf_op jit(solution)/shard_map/dot_general | solution.py:28
  363.8 21.9 %convert_reduce_fusion = (f32[2560]{0:T(1024)}, bf16[1600,2560]{1,0:T(8,128)(2,1)}) fusion(f32[1600,2560]{1,0:T(8,128)} %get-tuple-element.68, bf16[1600,640]{1,0:T(8,128)(2,1)S(1)} %get-tuple-element.60, bf16[3072,768]{1,0:T(8,128)(2,1)} %all-gather.17.cloned.1.call-done, f32[1600,2560]{1,0:T(8,128)} %get-tuple-element.76, ...), kind=kOutput, calls=%fused_computation.11 | convolution fusion | flops 5312509440 | bytes 46305280 | tf_op jit(solution)/shard_map/dot_general | solution.py:32
  385.7 14.5 %multiply_reduce_fusion.2 = (f32[640]{0:T(1024)S(1)}, f32[1600]{0:T(1024)S(1)}, f32[640]{0:T(1024)S(1)}, f32[1600,640]{1,0:T(8,128)S(1)}) fusion(f32[1600,640]{1,0:T(8,128)} %copy-done.5, f32[1600]{0:T(1024)S(1)} %fusion.60, f32[1600]{0:T(1024)S(1)} %broadcast_multiply_fusion.1, f32[640]{0:T(1024)S(1)} %get-tuple-element.93, f32[1600,640]{1,0:T(8,128)} %copy-done.7, ...), kind=kOutput, calls=%fused_computation.45 | convolution fusion | flops 5253117440 | bytes 23790080 | tf_op jit(solution)/shard_map/dot_general | solution.py:32
  415.3 7.9 reshape.147
  423.2 15.7 %convert_reduce_fusion.2 = (f32[10,64]{1,0:T(8,128)S(1)}, bf16[4,10,64,400]{3,2,1,0:T(8,128)(2,1)}) fusion(f32[4,10,400,400]{2,3,1,0:T(8,128)} %get-tuple-element.73, f32[4,10,400]{2,1,0:T(8,128)S(1)} %log_add_fusion, bf16[4,400,10,64]{1,0,3,2:T(4,128)(2,1)S(1)} %reshape.147), kind=kOutput, calls=%fused_computation.35 | convolution fusion | flops 841471360 | bytes 29762560 | tf_op jit(solution)/shard_map/bhqk,bqhd->bkhd/dot_general | solution.py:233
  444.3 6.0 convert_element_type.198
  456.5 25.4 %multiply_reduce_fusion = (f32[4,10,400]{2,1,0:T(8,128)S(1)}, f32[4,10,400,400]{2,3,1,0:T(8,128)}) fusion(f32[4,10,400,400]{2,3,1,0:T(8,128)} %get-tuple-element.73, f32[4,10,400]{2,1,0:T(8,128)S(1)} %log_add_fusion, bf16[4,400,10,64]{1,0,3,2:T(4,128)(2,1)} %reshape.144, bf16[4,400,10,64]{1,0,3,2:T(4,128)(2,1)S(1)} %reshape.147), kind=kOutput, calls=%fused_computation.1 | convolution fusion | flops 844784000 | bytes 55424000 | tf_op jit(solution)/shard_map/bqhd,bkhd->bhqk/dot_general | solution.py:230
  481.9 28.0 %multiply_convert_fusion = bf16[4,10,400,400]{2,3,1,0:T(8,128)(2,1)} fusion(f32[4,10,400,400]{2,3,1,0:T(8,128)} %get-tuple-element.81, f32[4,10,400,400]{2,3,1,0:T(8,128)} %get-tuple-element.73, f32[4,10,400]{2,1,0:T(8,128)S(1)} %get-tuple-element.80, f32[4,10,400]{2,1,0:T(8,128)S(1)} %log_add_fusion), kind=kLoop, calls=%fused_computation | loop fusion | flops 32000000 | bytes 64128000 | tf_op jit(solution)/shard_map/convert_element_type | solution.py:242
  510.0 8.7 fusion.24
  531.4 9.0 convert_reduce_fusion.3
  552.2 10.6 fusion.64
  569.3 9.9 fusion.83
  584.9 34.1 %reduce-scatter.9.cloned.1.call-done = f32[96,768]{1,0:T(8,128)} async-done(((f32[768,768]{1,0:T(8,128)}), f32[96,768]{1,0:T(8,128)}) %reduce-scatter.9.cloned.1.call-update) | async-done | bytes 294928 | tf_op jit(solution)/shard_map/reduce_scatter | solution.py:276
  619.1 71.4 %reduce-scatter.7.cloned.1.call-done = f32[96,768]{1,0:T(8,128)} async-done(((f32[768,768]{1,0:T(8,128)}), f32[96,768]{1,0:T(8,128)}) %reduce-scatter.7.cloned.1.call-update) | async-done | bytes 294928 | tf_op jit(solution)/shard_map/reduce_scatter | solution.py:275
  690.4 166.1 %reduce-scatter.15.cloned.1.call-done = f32[96,3072]{1,0:T(8,128)} async-done(((f32[768,3072]{1,0:T(8,128)}), f32[96,3072]{1,0:T(8,128)}) %reduce-scatter.15.cloned.1.call-update) | async-done | bytes 1179664 | tf_op jit(solution)/shard_map/reduce_scatter | solution.py:285
  856.5 165.9 %reduce-scatter.17.cloned.1.call-done = f32[384,768]{1,0:T(8,128)} async-done(((f32[3072,768]{1,0:T(8,128)}), f32[384,768]{1,0:T(8,128)}) %reduce-scatter.17.cloned.1.call-update) | async-done | bytes 1179664 | tf_op jit(solution)/shard_map/reduce_scatter | solution.py:287
  1022.5 5.9 fusion.50
  1032.6 6.7 select_convert_fusion
  1039.8 35.3 %all-reduce.35 = (f32[768]{0:T(1024)S(1)}, f32[768]{0:T(1024)S(1)}, f32[768]{0:T(1024)S(1)}, f32[768]{0:T(1024)S(1)}, f32[768]{0:T(1024)S(1)}, /*index=5*/f32[30...) all-reduce(f32[768]{0:T(1024)S(1)} %pad.57, ...), channel_id=6, replica_groups=mesh['dp'=4,'fsdp'=8] {'fsdp'}, use_global_device_ids=true, to_apply=%region_21.22.clone | all-reduce | flops 9984 | bytes 79872
  1075.8 7.0 all-reduce.36
  1082.8 17.6 %all-reduce.41.cloned.1.call-done = (f32[96,768]{1,0:T(8,128)}, f32[96,768]{1,0:T(8,128)}, f32[96,768]{1,0:T(8,128)}, f32[96,768]{1,0:T(8,128)}, f32[96,3072]{1,0:T(8,128)}, /*index=5*/f32[384,768]{1,0:T(8,128)}) async-done(((f32[96,768]{1,0:T(8,128)}, f32[96,768]{1,0:T(8,128)}, f32[96,768]{1,0:T(8,128)}, f32[96,768]{1,0:T(8,128)}, f32[96,3072]{1,0:T(8,128)}, /*index=5*/f32[384,768]{1,0:T(8,128)}), ...) | async-done | bytes 3538960 | tf_op jit(solution)/shard_map/psum | solution.py:273
  (224 shorter events, 160.5 us)
Async XLA Ops:
  7.2 65.3 %all-gather.7.cloned.1.call-start = ((), (), s32[]{:S(2)}) async-start(), calls=%async_computation.6 | async-start | bytes 1327104 | tf_op jit(solution)/shard_map/all_gather | solution.py:121
  7.9 88.4 %all-gather.9.cloned.1.call-start = ((), (), s32[]{:S(2)}) async-start(), calls=%async_computation.7 | async-start | bytes 1327104 | tf_op jit(solution)/shard_map/all_gather | solution.py:119
  8.7 129.7 %all-gather.11.cloned.1.call-start = ((), (), s32[]{:S(2)}) async-start(), calls=%async_computation.8 | async-start | bytes 1327104 | tf_op jit(solution)/shard_map/all_gather | solution.py:120
  9.4 196.6 %all-gather.13.cloned.1.call-start = ((), (), s32[]{:S(2)}) async-start(), calls=%async_computation.9 | async-start | bytes 1327104 | tf_op jit(solution)/shard_map/all_gather | solution.py:122
  10.0 251.0 %all-gather.15.cloned.1.call-start = ((), (), s32[]{:S(2)}) async-start(), calls=%async_computation.10 | async-start | bytes 5308416 | tf_op jit(solution)/shard_map/all_gather | solution.py:162
  10.6 330.5 %all-gather.17.cloned.1.call-start = ((), (), s32[]{:S(2)}) async-start(), calls=%async_computation.11 | async-start | bytes 5308416 | tf_op jit(solution)/shard_map/all_gather | solution.py:164
  10.6 50.5 %collective-permute-start = (bf16[384]{0:T(512)(128)(2,1)}, bf16[384]{0:T(512)(128)(2,1)S(1)}, u32[]{:S(2)}, u32[]{:S(2)}) collective-permute-start(bf16[384]{0:T(512)(128)(2,1)} %param.32), channel_id=1, source_target_pairs={{0,7},{1,0},{2,1},{3,2},{4,3},{5,4},{6,5},{7,6},{8,15},{9,8},{10,9... | collective-permute-start | bytes 2312 | tf_op jit(solution)/shard_map/ppermute | solution.py:20
  16.7 568.2 %reduce-scatter.13.cloned.1.call-start = ((), (), s32[]{:S(2)}) async-start(), calls=%async_computation.15 | async-start | bytes 2654208 | tf_op jit(solution)/shard_map/reduce_scatter | solution.py:278
  59.8 146.2 %copy-start.34 = (f32[640]{0:T(1024)}, f32[640]{0:T(1024)S(1)}, u32[]{:S(2)}) copy-start(f32[640]{0:T(1024)S(1)} %slice_convert_fusion.8) | copy-start | bytes 7684
  59.9 281.2 %copy-start.32 = (f32[640]{0:T(1024)}, f32[640]{0:T(1024)S(1)}, u32[]{:S(2)}) copy-start(f32[640]{0:T(1024)S(1)} %get-tuple-element.92) | copy-start | bytes 7684
  61.8 3.7 collective-permute-start.1
  66.2 4.5 collective-permute-start.2
  67.1 138.9 %copy-start.25 = (pred[1600]{0:T(1024)(128)(4,1)}, pred[1600]{0:T(1024)(128)(4,1)S(1)}, u32[]{:S(2)}) copy-start(pred[1600]{0:T(1024)(128)(4,1)S(1)} %broadcast_in_dim.36) | copy-start | bytes 4804
  152.9 15.4 %copy-start.2 = (bf16[4,400,10,64]{1,0,3,2:T(4,128)(2,1)}, bf16[4,400,10,64]{1,0,3,2:T(4,128)(2,1)S(1)}, u32[]{:S(2)}) copy-start(bf16[4,400,10,64]{1,0,3,2:T(4,128)(2,1)S(1)} %reshape.146) | copy-start | bytes 6144004
  168.3 14.0 %copy-start.16 = (f32[4,10,400]{2,1,0:T(8,128)}, f32[4,10,400]{2,1,0:T(8,128)S(1)}, u32[]{:S(2)}) copy-start(f32[4,10,400]{2,1,0:T(8,128)S(1)} %get-tuple-element.72) | copy-start | bytes 192004
  168.3 14.0 %copy-start.8 = (bf16[4,400,10,64]{1,0,3,2:T(4,128)(2,1)S(1)}, bf16[4,400,10,64]{1,0,3,2:T(4,128)(2,1)}, u32[]{:S(2)}) copy-start(bf16[4,400,10,64]{1,0,3,2:T(4,128)(2,1)} %reshape.144) | copy-start | bytes 6144004
  182.3 16.0 %copy-start.20 = (f32[4,10,400]{2,1,0:T(8,128)}, f32[4,10,400]{2,1,0:T(8,128)S(1)}, u32[]{:S(2)}) copy-start(f32[4,10,400]{2,1,0:T(8,128)S(1)} %fusion) | copy-start | bytes 192004
  261.0 80.1 %copy-start.36 = (f32[640]{0:T(1024)S(1)}, f32[640]{0:T(1024)}, u32[]{:S(2)}) copy-start(f32[640]{0:T(1024)} %slice_convert_fusion.2) | copy-start | bytes 7684
  363.8 21.9 %copy-start.13 = (bf16[1600,640]{1,0:T(8,128)(2,1)}, bf16[1600,640]{1,0:T(8,128)(2,1)S(1)}, u32[]{:S(2)}) copy-start(bf16[1600,640]{1,0:T(8,128)(2,1)S(1)} %get-tuple-element.60) | copy-start | bytes 6144004
  385.7 14.5 %copy-start.23 = (f32[1600]{0:T(1024)S(1)}, f32[1600]{0:T(1024)}, u32[]{:S(2)}) copy-start(f32[1600]{0:T(1024)} %copy-done.22) | copy-start | bytes 19204
  385.7 14.6 %copy-start.6 = (f32[1600,640]{1,0:T(8,128)S(1)}, f32[1600,640]{1,0:T(8,128)}, u32[]{:S(2)}) copy-start(f32[1600,640]{1,0:T(8,128)} %copy-done.5) | copy-start | bytes 12288004
  408.7 176.3 %reduce-scatter.11.cloned.1.call-start = ((), (), s32[]{:S(2)}) async-start(), calls=%async_computation.14 | async-start | bytes 2654208 | tf_op jit(solution)/shard_map/reduce_scatter | solution.py:277
  438.9 11.4 %copy-start.26 = (pred[1600]{0:T(1024)(128)(4,1)S(1)}, pred[1600]{0:T(1024)(128)(4,1)}, u32[]{:S(2)}) copy-start(pred[1600]{0:T(1024)(128)(4,1)} %copy-done.25) | copy-start | bytes 4804
  438.9 11.4 %copy-start.35 = (f32[640]{0:T(1024)S(1)}, f32[640]{0:T(1024)}, u32[]{:S(2)}) copy-start(f32[640]{0:T(1024)} %copy-done.34) | copy-start | bytes 7684
  456.4 162.6 %reduce-scatter.9.cloned.1.call-start = ((), (), s32[]{:S(2)}) async-start(), calls=%async_computation.13 | async-start | bytes 2654208 | tf_op jit(solution)/shard_map/reduce_scatter | solution.py:276
  481.9 28.1 %copy-start.4 = (bf16[4,400,10,64]{1,0,3,2:T(4,128)(2,1)S(1)}, bf16[4,400,10,64]{1,0,3,2:T(4,128)(2,1)}, u32[]{:S(2)}) copy-start(bf16[4,400,10,64]{1,0,3,2:T(4,128)(2,1)} %reshape.145) | copy-start | bytes 6144004
  530.4 160.0 %reduce-scatter.7.cloned.1.call-start = ((), (), s32[]{:S(2)}) async-start(), calls=%async_computation.12 | async-start | bytes 2654208 | tf_op jit(solution)/shard_map/reduce_scatter | solution.py:275
  552.2 304.3 %reduce-scatter.15.cloned.1.call-start = ((), (), s32[]{:S(2)}) async-start(), calls=%async_computation.16 | async-start | bytes 10616832 | tf_op jit(solution)/shard_map/reduce_scatter | solution.py:285
  567.7 454.7 %reduce-scatter.17.cloned.1.call-start = ((), (), s32[]{:S(2)}) async-start(), calls=%async_computation.17 | async-start | bytes 10616832 | tf_op jit(solution)/shard_map/reduce_scatter | solution.py:287
  583.5 516.9 %all-reduce.41.cloned.1.call-start = ((), (), s32[]{:S(2)}) async-start(), calls=%async_computation.18 | async-start | bytes 7077888 | tf_op jit(solution)/shard_map/psum | solution.py:273
  1022.5 6.1 copy-start.11
  1100.4 9.2 copy-start.18
  (21 other events, 67.8 us)
Sparse Core Ops, SparseCore 0:
  10.2 43.9 all-gather.6
  56.4 39.8 all-gather.8
  98.5 39.8 all-gather.10
  140.4 39.8 all-gather.12
  182.3 78.6 all-gather.14
  263.0 78.0 all-gather.16
  408.8 67.1 reduce-scatter.12
  479.5 68.0 reduce-scatter.10
  551.0 67.9 reduce-scatter.8
  622.4 67.9 reduce-scatter.6
  694.0 162.4 reduce-scatter.14
  860.0 162.3 reduce-scatter.16
  1025.2 75.1 all-reduce.40
